TPU v7x, 32 devices: a whole 2x2x4 slice. The times are simulated.
32 devices in a mesh: dp: 2 (over x), ctx: 4 (over y, core), head: 4 (over z).
Axes of the slice: x: 2, y: 2, z: 4, core: 2. Of those that a mesh axis runs over, the one named last changes fastest.
Arguments:
- tokens: bfloat16 [2, 1024, 2048], P('dp', 'ctx'), may hold values from -6 to 6
- proj_weights: bfloat16 [3, 2048, 1024], P(None, None, 'head'), may hold values from -0.125 to 0.125
- init_weight: float32 [8, 128, 128], P('head'), may hold values from -0.5 to 0.5
- base_rates: float32 [8], P('head'), may hold values from 0.005 to 1
- gate_values: float32 [2, 8, 1024], P('dp', 'head', 'ctx'), may hold values from 0.3 to 480
- out_gain: float32 [8, 128], P('head'), may hold values from 0.5 to 1.5
- cotangent: bfloat16 [2, 1024, 1024], P('dp', 'ctx', 'head'), may hold values from -6 to 6
Outputs:
- grad_tokens: bfloat16 [2, 1024, 2048], P('dp', 'ctx', 'head')
- grad_proj: float32 [3, 2048, 1024], P(None, None, 'head')
- grad_init: float32 [8, 128, 128], P('head')
- grad_gain: float32 [8, 128], P('head')
- grad_rates: float32 [8], P('head')
- grad_gates: float32 [2, 8, 1024], P('dp', 'head', 'ctx')
All inputs are finite; a program needn't handle non-finite values.
Results may differ from a plain program's by a relative error of at most 0.0072.
Values sent between devices are 32-bit elements; how exact they have to be, the bound alone decides.
A program may use at most 64 MiB of HBM per device.

v0:
```python
import functools

import jax
import jax.numpy as jnp
from jax import lax
from jax.experimental import pallas as pl
from jax.experimental.pallas import tpu as pltpu
from jax.sharding import PartitionSpec as P

MB = 16
F32 = jnp.float32
BF16 = jnp.bfloat16
MESH = pl.DeviceIdType.MESH


def split(x):
    if x.dtype == BF16:
        return (x, None)
    high = x.astype(BF16)
    return (high, (x - high.astype(F32)).astype(BF16))


def dot(left, right, dims=(1, 0)):
    def one(a, b):
        return lax.dot_general(a, b, (((dims[0],), (dims[1],)), ((), ())), preferred_element_type=F32)

    total = one(left[0], right[0])
    if right[1] is not None:
        total = total + one(left[0], right[1])
    if left[1] is not None:
        total = total + one(left[1], right[0])
    return total


def pair(parts):
    return tuple(jnp.concatenate(p, axis=1) for p in zip(*parts))


def grid_index(count):
    rows = lax.broadcasted_iota(jnp.int32, (count, count), 0)
    columns = lax.broadcasted_iota(jnp.int32, (count, count), 1)
    return rows, columns


def to_column(row, rows, columns):
    return jnp.sum(jnp.where(rows == columns, row, 0.0), axis=1, keepdims=True)


def to_row(column, rows, columns):
    return jnp.sum(jnp.where(rows == columns, column, 0.0), axis=0, keepdims=True)


def prepare(queries, raw_keys, values, base, gate_row):
    count = queries.shape[0]
    rows, columns = grid_index(count)
    raw = raw_keys.astype(F32)
    norm_inv = lax.rsqrt(jnp.sum(raw * raw, axis=1, keepdims=True) + 1e-06)
    keys = raw * norm_inv
    boost_row = base * gate_row
    rate_row = boost_row / (1.0 + boost_row)
    rate = to_column(rate_row, rows, columns)
    keys_s = split(keys)
    gram = dot(keys_s, keys_s, (1, 1))
    row_block, column_block = rows // MB, columns // MB
    lower = gram * rate_row
    near = (row_block // 2 == column_block // 2) & (row_block > column_block)
    inverse = jnp.where(rows == columns, 1.0, 0.0) - jnp.where(near, lower, 0.0)
    size = 2
    while size * MB < count:
        here = (
            (row_block // (2 * size) == column_block // (2 * size))
            & (row_block // size > column_block // size)
        )
        inverse_s = split(inverse)
        middle = split(dot(inverse_s, split(jnp.where(here, lower, 0.0))))
        inverse = inverse - dot(middle, inverse_s)
        size *= 2
    inverse_s = split(inverse)
    solved = dot(inverse_s, (jnp.concatenate([values, keys_s[0]], 1), jnp.concatenate([jnp.zeros_like(values), keys_s[1]], 1)))
    solved_s = split(solved)
    rate_keys_s = split(rate * keys)
    ends = dot(rate_keys_s, solved_s, (0, 0))
    return dict(
        norm_inv=norm_inv, keys=keys, keys_s=keys_s, boost_row=boost_row, rate=rate, rate_row=rate_row,
        inverse_s=inverse_s, solved=solved, solved_s=solved_s, ends=ends, rate_keys_s=rate_keys_s,
    )


def reach_out(queries, state):
    count, width = queries.shape
    rows, columns = grid_index(count)
    scores = jnp.where(rows >= columns, dot((queries, None), state["keys_s"], (1, 1)), 0.0)
    mixed = dot(split(scores * state["rate_row"]), state["solved_s"])
    state["scores_s"] = split(scores)
    state["reach_s"] = split(queries.astype(F32) - mixed[:, width:])
    state["own_out"] = mixed[:, :width]
    state["pull_s"] = split(dot(state["inverse_s"], state["rate_keys_s"], (0, 0)))


def forward(start, gain, upstream, state):
    width = start.shape[0]
    start_s = split(start)
    inner_out = state["own_out"] + dot(state["reach_s"], start_s)
    solved_keys = (state["solved_s"][0][:, width:], state["solved_s"][1][:, width:])
    state["residual"] = state["solved"][:, :width] - dot(solved_keys, start_s)
    centred = inner_out - jnp.mean(inner_out, axis=1, keepdims=True)
    inv_std = lax.rsqrt(jnp.mean(centred * centred, axis=1, keepdims=True) + 1e-05)
    normed = centred * inv_std
    weighted = upstream * gain
    d_out = inv_std * (
        weighted
        - jnp.mean(weighted, axis=1, keepdims=True)
        - normed * jnp.mean(weighted * normed, axis=1, keepdims=True)
    )
    state["start_s"] = start_s
    state["d_out_s"] = split(d_out)
    state["d_gain"] = jnp.sum(upstream * normed, axis=0, keepdims=True)
    return dot(state["reach_s"], state["d_out_s"], (0, 0))


def query_grad(queries, upstream, state):
    rows, columns = grid_index(queries.shape[0])
    state["rate_res_s"] = split(state["rate"] * state["residual"])
    d_scores = jnp.where(rows >= columns, dot(state["d_out_s"], state["rate_res_s"], (1, 1)), 0.0)
    d_scores_s = split(d_scores)
    d_queries = upstream + dot(state["d_out_s"], state["start_s"], (1, 1)) + dot(d_scores_s, state["keys_s"])
    state["d_scores_s"] = d_scores_s
    return d_queries


def before_end(queries, state):
    state["from_scores"] = dot(state["d_scores_s"], (queries, None), (0, 0))
    pushed = state["rate"] * dot(state["scores_s"], state["d_out_s"], (0, 0))
    state["d_val"] = dot(state["inverse_s"], split(pushed), (0, 0))


def key_value_grad(end_grad, base, gate_row, state):
    rows, columns = grid_index(state["keys"].shape[0])
    end_s = split(end_grad)
    d_val = state["d_val"] + dot(state["pull_s"], end_s)
    d_val_s = split(d_val)
    strict = rows // MB > columns // MB
    d_lower = jnp.where(strict, dot(d_val_s, state["rate_res_s"], (1, 1)), 0.0)
    d_gram_s = split(d_lower + d_lower.T)
    d_keys = (
        state["from_scores"]
        - dot(d_val_s, state["start_s"], (1, 1))
        + dot(state["rate_res_s"], end_s, (1, 1))
        - dot(d_gram_s, state["keys_s"])
    )
    keys = state["keys"]
    d_raw = state["norm_inv"] * (d_keys - keys * jnp.sum(keys * d_keys, axis=1, keepdims=True))
    d_rate = jnp.sum(state["residual"] * d_val, axis=1, keepdims=True) / state["rate"]
    boost = state["boost_row"]
    d_boost = to_row(d_rate, rows, columns) / ((1.0 + boost) * (1.0 + boost))
    return d_raw, d_val, d_boost * base, jnp.sum(d_boost * gate_row, axis=1, keepdims=True)


def kernel(
    sizes,
    tok_ref, w_ref, init_ref, rates_ref, gate_ref, gain_ref, cot_ref,
    gt_out, proj_out, ext_out, gates_out,
    tok_t, maps, maps_all, pulls, pulls_all, acc, ext, full, ext_full, landing, ext_landing, part, part_in,
    maps_send, maps_recv, pulls_send, pulls_recv, part_send, part_recv, red_send, red_recv, done_sem,
):
    n_dp, n_ctx, n_head = sizes
    count, model = tok_ref.shape
    heads, width, _ = init_ref.shape
    dp, ctx, head = lax.axis_index("dp"), lax.axis_index("ctx"), lax.axis_index("head")
    place = {"dp": dp, "ctx": ctx}

    def flip(axis, bit):
        step = 1 << bit
        mine = lax.rem(place[axis] // step, 2)
        return mine, place[axis] + step - 2 * step * mine

    dp_bits = [("dp", b) for b in range(n_dp.bit_length() - 1)]
    ctx_bits = [("ctx", b) for b in range(n_ctx.bit_length() - 1)]
    orders = (ctx_bits + dp_bits, ctx_bits[:1] + dp_bits + ctx_bits[1:])
    stages = len(orders[0])

    barrier = pltpu.get_barrier_semaphore()
    for off in range(1, n_ctx):
        pl.semaphore_signal(barrier, inc=1, device_id={"ctx": lax.rem(ctx + off, n_ctx)}, device_id_type=MESH)
    for off in range(1, n_head):
        pl.semaphore_signal(barrier, inc=1, device_id={"head": lax.rem(head + off, n_head)}, device_id_type=MESH)
    for axis, bit in dp_bits:
        pl.semaphore_signal(barrier, inc=1, device_id={axis: flip(axis, bit)[1]}, device_id_type=MESH)

    tokens = tok_ref[...]
    projected = [
        jnp.dot(tokens, w_ref[which], preferred_element_type=F32).astype(BF16) for which in range(3)
    ]
    span = [slice(h * width, (h + 1) * width) for h in range(heads)]
    queries = [projected[0][:, s] for s in span]
    states = []
    rows, columns = grid_index(width)
    eye = jnp.where(rows == columns, 1.0, 0.0)
    for h in range(heads):
        state = prepare(
            queries[h], projected[1][:, span[h]], projected[2][:, span[h]], rates_ref[h], gate_ref[0, h : h + 1, :]
        )
        states.append(state)
        maps[h, 0] = eye - state["ends"][:, width:]
        maps[h, 1] = state["ends"][:, :width]

    pl.semaphore_wait(barrier, (n_ctx - 1) + (n_head - 1) + len(dp_bits))

    def share(block, slots, send, recv):
        slots[pl.ds(ctx, 1)] = block[...][None]
        copies = []
        for off in range(1, n_ctx):
            copy = pltpu.make_async_remote_copy(
                src_ref=block, dst_ref=slots.at[ctx], send_sem=send.at[off - 1], recv_sem=recv.at[off - 1],
                device_id={"ctx": lax.rem(ctx + off, n_ctx)}, device_id_type=MESH,
            )
            copy.start()
            copies.append(copy)
        return copies

    copies = share(maps, maps_all, maps_send, maps_recv)
    for h in range(heads):
        reach_out(queries[h], states[h])
    tok_t[...] = tokens.T
    for copy in copies:
        copy.wait()

    upstreams = []
    for h in range(heads):
        start = init_ref[h]
        for i in range(n_ctx - 1):
            moved = dot(split(maps_all[i, h, 0]), split(start)) + maps_all[i, h, 1]
            start = jnp.where(ctx > i, moved, start)
        upstream = cot_ref[:, span[h]].astype(F32)
        upstreams.append(upstream)
        pulls[h] = forward(start, gain_ref[h : h + 1, :], upstream, states[h])
    copies = share(pulls, pulls_all, pulls_send, pulls_recv)

    half = model // 2
    work = [(which * 2 + part_, acc, full, landing, (which * 2 + part_) * half, half, orders[part_]) for which in range(3) for part_ in range(2)]
    work.append((6, ext, ext_full, ext_landing, 0, ext.shape[0], orders[0]))
    at = {item[0]: item[4] for item in work}
    flight = {}

    def reduce_start(item, stage):
        number, source, _, land, base, length, order = item
        axis, bit = order[stage]
        mine, partner = flip(axis, bit)
        length = length >> (stage + 1)
        slot = (0 if number == 6 else number * half) + (item[5] - (item[5] >> stage))
        away = pl.multiple_of(at[number] + (1 - mine) * length, 8)
        copy = pltpu.make_async_remote_copy(
            src_ref=source.at[pl.ds(away, length)], dst_ref=land.at[pl.ds(slot, length)],
            send_sem=red_send.at[number, stage], recv_sem=red_recv.at[number, stage],
            device_id={axis: partner}, device_id_type=MESH,
        )
        copy.start()
        flight[number] = (copy, slot, length)
        at[number] = pl.multiple_of(at[number] + mine * length, 8)

    def reduce_end(item, stage):
        number, source, target, land = item[:4]
        copy, slot, length = flight[number]
        copy.wait()
        total = source[pl.ds(at[number], length)] + land[pl.ds(slot, length)]
        (target if stage == stages - 1 else source)[pl.ds(at[number], length)] = total

    def gather_start(item, stage):
        number, _, target, _, _, length, order = item
        axis, bit = order[stage]
        mine, partner = flip(axis, bit)
        length = length >> (stage + 1)
        window = target.at[pl.ds(at[number], length)]
        copy = pltpu.make_async_remote_copy(
            src_ref=window, dst_ref=window,
            send_sem=red_send.at[number, 2 * stages - 1 - stage], recv_sem=red_recv.at[number, 2 * stages - 1 - stage],
            device_id={axis: partner}, device_id_type=MESH,
        )
        copy.start()
        flight[number] = (copy, None, None)
        at[number] = pl.multiple_of(at[number] - mine * length, 8)

    def project(which, grads):
        grad = jnp.concatenate(grads, axis=1).astype(BF16)
        for part_ in range(2):
            where = pl.ds((which * 2 + part_) * half, half)
            acc[where] = jnp.dot(tok_t[pl.ds(part_ * half, half)], grad, preferred_element_type=F32)
            reduce_start(work[which * 2 + part_], 0)
        return grad

    d_rows = [None] * 3
    d_rows[0] = project(0, [query_grad(queries[h], upstreams[h], states[h]) for h in range(heads)])
    for h in range(heads):
        before_end(queries[h], states[h])
    for copy in copies:
        copy.wait()

    results = []
    ext[...] = jnp.zeros_like(ext)
    for h in range(heads):
        grad = jnp.zeros((width, width), F32)
        end_grad = grad
        for i in reversed(range(n_ctx)):
            end_grad = jnp.where(ctx == i, grad, end_grad)
            grad = dot(split(maps_all[i, h, 0]), split(grad), (0, 0)) + pulls_all[i, h]
        ext[0:width, span[h]] = jnp.where(ctx == 0, grad, 0.0)
        d_raw, d_val, gates, d_base = key_value_grad(end_grad, rates_ref[h], gate_ref[0, h : h + 1, :], states[h])
        results.append((d_raw, d_val))
        gates_out[0, h : h + 1, :] = gates
        ext[width : width + 1, span[h]] = states[h]["d_gain"]
        ext[width + 8 : width + 9, span[h]] = jnp.broadcast_to(d_base, (1, width))
    d_rows[1] = project(1, [r[0] for r in results])
    d_rows[2] = project(2, [r[1] for r in results])
    reduce_start(work[6], 0)

    share_ = model // n_head

    def token_part(which_head):
        total = None
        for which in range(3):
            weight = w_ref[which, pl.ds(pl.multiple_of(which_head * share_, share_), share_), :]
            term = lax.dot_general(d_rows[which], weight, (((1,), (1,)), ((), ())), preferred_element_type=F32)
            total = term if total is None else total + term
        return total

    part_copies = []
    for off in range(1, n_head):
        to = lax.rem(head + off, n_head)
        part[off - 1] = token_part(to)
        copy = pltpu.make_async_remote_copy(
            src_ref=part.at[off - 1], dst_ref=part_in.at[off - 1],
            send_sem=part_send.at[off - 1], recv_sem=part_recv.at[off - 1],
            device_id={"head": to}, device_id_type=MESH,
        )
        copy.start()
        part_copies.append(copy)
    own_part = token_part(head)

    for stage in range(stages):
        for item in work:
            reduce_end(item, stage)
            if stage + 1 < stages:
                reduce_start(item, stage + 1)
            else:
                gather_start(item, stage)
    for stage in reversed(range(stages - 1)):
        for item in work:
            flight[item[0]][0].wait()
            gather_start(item, stage)
    for copy in part_copies:
        copy.wait()
    for off in range(1, n_head):
        own_part = own_part + part_in[off - 1]
    gt_out[...] = own_part.astype(BF16)
    outs = []
    for item in work:
        number, _, target, _, base, length, _ = item
        flight[number][0].wait()
        if number < 6:
            copy = pltpu.make_async_copy(target.at[pl.ds(base, length)], proj_out.at[pl.ds(base, length)], done_sem.at[number])
            copy.start()
            outs.append(copy)
        else:
            ext_out[...] = ext_full[...]
    for copy in outs:
        copy.wait()


def body(sizes, tokens, proj_weights, init_weight, base_rates, gate_values, out_gain, cotangent):
    flattened = tokens.reshape(-1, tokens.shape[-1])
    count, model = flattened.shape
    heads, width, _ = init_weight.shape
    n_dp, n_ctx, n_head = sizes
    stages = (n_dp * n_ctx).bit_length() - 1
    span = heads * width
    ext_rows = 256
    vmem, dma = pltpu.VMEM, pltpu.SemaphoreType.DMA
    in_vmem = pl.BlockSpec(memory_space=vmem)
    tokens_grad, proj, ext, gates = pl.pallas_call(
        functools.partial(kernel, sizes),
        out_shape=(
            jax.ShapeDtypeStruct((count, model // n_head), BF16),
            jax.ShapeDtypeStruct((3 * model, span), F32),
            jax.ShapeDtypeStruct((ext_rows, span), F32),
            jax.ShapeDtypeStruct(gate_values.shape, F32),
        ),
        in_specs=[in_vmem] * 3 + [pl.BlockSpec(memory_space=pltpu.SMEM)] + [in_vmem] * 3,
        out_specs=(in_vmem, pl.BlockSpec(memory_space=pl.ANY), in_vmem, in_vmem),
        scratch_shapes=[
            vmem((model, count), BF16),
            vmem((heads, 2, width, width), F32),
            vmem((n_ctx, heads, 2, width, width), F32),
            vmem((heads, width, width), F32),
            vmem((n_ctx, heads, width, width), F32),
            vmem((3 * model, span), F32),
            vmem((ext_rows, span), F32),
            vmem((3 * model, span), F32),
            vmem((ext_rows, span), F32),
            vmem((3 * model, span), F32),
            vmem((ext_rows, span), F32),
            vmem((n_head - 1, count, model // n_head), F32),
            vmem((n_head - 1, count, model // n_head), F32),
            dma((n_ctx - 1,)), dma((n_ctx - 1,)), dma((n_ctx - 1,)), dma((n_ctx - 1,)),
            dma((n_head - 1,)), dma((n_head - 1,)),
            dma((7, 2 * stages)), dma((7, 2 * stages)), dma((6,)),
        ],
        compiler_params=pltpu.CompilerParams(
            collective_id=0, has_side_effects=True, vmem_limit_bytes=56 * 1024 * 1024
        ),
        cost_estimate=pl.CostEstimate(flops=4_000_000_000, bytes_accessed=12_000_000, transcendentals=0),
    )(
        flattened, proj_weights, init_weight, base_rates, gate_values, out_gain,
        cotangent.reshape(count, span),
    )
    grad_init = jnp.stack([ext[:width, h * width : (h + 1) * width] for h in range(heads)])
    grad_gain = ext[width].reshape(heads, width)
    grad_rates = ext[width + 8].reshape(heads, width)[:, 0]
    return (
        tokens_grad[None], proj.reshape(3, model, span), grad_init, grad_gain, grad_rates, gates,
    )


def solution(mesh):
    sizes = (mesh.shape["dp"], mesh.shape["ctx"], mesh.shape["head"])
    in_specs = (
        P("dp", "ctx", None),
        P(None, None, "head"),
        P("head", None, None),
        P("head"),
        P("dp", "head", "ctx"),
        P("head", None),
        P("dp", "ctx", "head"),
    )
    out_specs = (
        P("dp", "ctx", "head"),
        P(None, None, "head"),
        P("head", None, None),
        P("head", None),
        P("head"),
        P("dp", "head", "ctx"),
    )
    return jax.shard_map(
        functools.partial(body, sizes), mesh=mesh, in_specs=in_specs, out_specs=out_specs, check_vma=False
    )
```

profile of v0, /device:TPU:0, one launch (start us, length us, event | category | flops | bytes accessed | tf_op | source)
XLA Modules:
  0.0 109.3 jit_solution(4483640744049897434)
XLA Ops:
  0.6 97.1 %shard_map.118 = (bf16[256,512]{1,0:T(8,128)(2,1)}, f32[6144,256]{1,0:T(8,128)}, f32[256,256]{1,0:T(8,128)}, f32[1,2,256]{2,1,0:T(2,128)}) custom-call(bf16[256,2048]{1,0:T(8,128)(2,1)} %bitcast.16, bf16[3,2048,256]{2,1,0:T(8,128)(2,1)} %w_ref.1, f32[2,128,128]{2,1,0:T(8,128)} %init_ref.1, f32[2]{0:T(128)} %rates_ref.1, f32[1,2,256]{2,1,0:T(2,128)} %gate_ref.1, ...), custom_call_target="tpu_custom_call" | custom-call | flops 4000000000 | bytes 12000000 | tf_op jit(solution)/shard_map/pallas_call | solution.py:379
  97.8 0.9 slice_bitcast_fusion.1
  98.6 0.7 pad_maximum_fusion
  99.3 1.3 %fusion = (f32[1,256]{1,0:T(1,128)S(1)}, f32[1,256]{1,0:T(1,128)}) fusion(f32[256,256]{1,0:T(8,128)} %get-tuple-element.12), kind=kLoop, calls=%fused_computation.3 | loop fusion | bytes 4096 | tf_op jit(solution)/shard_map/slice | solution.py:417
  100.6 0.6 copy.14
  101.2 1.7 %copy.18 = bf16[1,256,512]{2,1,0:T(8,128)(2,1)} copy(bf16[1,256,512]{2,1,0:T(8,128)(2,1)} %bitcast.13) | data formatting | bytes 524288
  102.8 0.0 copy-start
  102.8 5.9 %copy.19 = f32[3,2048,256]{2,1,0:T(8,128)} copy(f32[3,2048,256]{2,1,0:T(8,128)} %bitcast.12) | data formatting | bytes 12582912
  108.7 0.0 copy-done
  108.7 0.6 copy.20
Async XLA Ops:
  102.8 5.9 %copy-start = (f32[1,2,256]{2,1,0:T(2,128)S(1)}, f32[1,2,256]{2,1,0:T(2,128)}, u32[]{:S(2)}) copy-start(f32[1,2,256]{2,1,0:T(2,128)} %get-tuple-element.29) | copy-start | bytes 6148
where the time goes:
time: 110 us; the launch traced here: 109 us
  Pallas kernels  97.1 us (88%)
  local copies, waits for them, and re-layouts  10.9 us (10%)
    pallas_call x1, Pallas kernels, body(): pl.pallas_call(functools.partial(kernel, sizes), out_shape=(jax.ShapeDtyp...  97.1 us
    unnamed x6, local copies, waits for them, and re-layouts  8.74 us

commit v1 on v0

--- a/solution.py
+++ b/solution.py
@@ -32,8 +32,17 @@
     return total
 
 
-def pair(parts):
-    return tuple(jnp.concatenate(p, axis=1) for p in zip(*parts))
+def together(steps):
+    results = [None] * len(steps)
+    open_ = list(range(len(steps)))
+    while open_:
+        for at in list(open_):
+            try:
+                next(steps[at])
+            except StopIteration as end:
+                results[at] = end.value
+                open_.remove(at)
+    return results
 
 
 def grid_index(count):
@@ -61,22 +70,47 @@
     rate = to_column(rate_row, rows, columns)
     keys_s = split(keys)
     gram = dot(keys_s, keys_s, (1, 1))
-    row_block, column_block = rows // MB, columns // MB
-    lower = gram * rate_row
-    near = (row_block // 2 == column_block // 2) & (row_block > column_block)
-    inverse = jnp.where(rows == columns, 1.0, 0.0) - jnp.where(near, lower, 0.0)
+    yield
+    lower = jnp.where(rows // MB > columns // MB, gram * rate_row, 0.0)
+    tile = min(count, 128)
+    tile_rows, tile_columns = grid_index(tile)
+    row_block, column_block = tile_rows // MB, tile_columns // MB
+    eye = jnp.where(tile_rows == tile_columns, 1.0, 0.0)
+    tiles = count // tile
+    lowers = [lower[t * tile : (t + 1) * tile, t * tile : (t + 1) * tile] for t in range(tiles)]
+    near = row_block // 2 == column_block // 2
+    inverses = [eye - jnp.where(near, low, 0.0) for low in lowers]
     size = 2
-    while size * MB < count:
+    while size * MB < tile:
         here = (
             (row_block // (2 * size) == column_block // (2 * size))
             & (row_block // size > column_block // size)
         )
-        inverse_s = split(inverse)
-        middle = split(dot(inverse_s, split(jnp.where(here, lower, 0.0))))
-        inverse = inverse - dot(middle, inverse_s)
+        inverses_s = [split(inv) for inv in inverses]
+        middles = [dot(inv, split(jnp.where(here, low, 0.0))) for inv, low in zip(inverses_s, lowers)]
+        yield
+        inverses = [inv - dot(split(mid), inv_s) for inv, mid, inv_s in zip(inverses, middles, inverses_s)]
+        yield
         size *= 2
-    inverse_s = split(inverse)
+    size = tile
+    while size < count:
+        joined = []
+        for t in range(0, len(inverses), 2):
+            low = lower[(t + 1) * size : (t + 2) * size, t * size : (t + 1) * size]
+            first_s, second_s = split(inverses[t]), split(inverses[t + 1])
+            middle = dot(second_s, split(low))
+            yield
+            corner = -dot(split(middle), first_s)
+            yield
+            joined.append(jnp.concatenate([
+                jnp.concatenate([inverses[t], jnp.zeros((size, size), F32)], 1),
+                jnp.concatenate([corner, inverses[t + 1]], 1),
+            ], 0))
+        inverses = joined
+        size *= 2
+    inverse_s = split(inverses[0])
     solved = dot(inverse_s, (jnp.concatenate([values, keys_s[0]], 1), jnp.concatenate([jnp.zeros_like(values), keys_s[1]], 1)))
+    yield
     solved_s = split(solved)
     rate_keys_s = split(rate * keys)
     ends = dot(rate_keys_s, solved_s, (0, 0))
@@ -90,7 +124,9 @@
     count, width = queries.shape
     rows, columns = grid_index(count)
     scores = jnp.where(rows >= columns, dot((queries, None), state["keys_s"], (1, 1)), 0.0)
+    yield
     mixed = dot(split(scores * state["rate_row"]), state["solved_s"])
+    yield
     state["scores_s"] = split(scores)
     state["reach_s"] = split(queries.astype(F32) - mixed[:, width:])
     state["own_out"] = mixed[:, :width]
@@ -101,8 +137,10 @@
     width = start.shape[0]
     start_s = split(start)
     inner_out = state["own_out"] + dot(state["reach_s"], start_s)
+    yield
     solved_keys = (state["solved_s"][0][:, width:], state["solved_s"][1][:, width:])
     state["residual"] = state["solved"][:, :width] - dot(solved_keys, start_s)
+    yield
     centred = inner_out - jnp.mean(inner_out, axis=1, keepdims=True)
     inv_std = lax.rsqrt(jnp.mean(centred * centred, axis=1, keepdims=True) + 1e-05)
     normed = centred * inv_std
@@ -122,15 +160,19 @@
     rows, columns = grid_index(queries.shape[0])
     state["rate_res_s"] = split(state["rate"] * state["residual"])
     d_scores = jnp.where(rows >= columns, dot(state["d_out_s"], state["rate_res_s"], (1, 1)), 0.0)
+    yield
     d_scores_s = split(d_scores)
     d_queries = upstream + dot(state["d_out_s"], state["start_s"], (1, 1)) + dot(d_scores_s, state["keys_s"])
+    yield
     state["d_scores_s"] = d_scores_s
     return d_queries
 
 
 def before_end(queries, state):
     state["from_scores"] = dot(state["d_scores_s"], (queries, None), (0, 0))
+    yield
     pushed = state["rate"] * dot(state["scores_s"], state["d_out_s"], (0, 0))
+    yield
     state["d_val"] = dot(state["inverse_s"], split(pushed), (0, 0))
 
 
@@ -138,9 +180,11 @@
     rows, columns = grid_index(state["keys"].shape[0])
     end_s = split(end_grad)
     d_val = state["d_val"] + dot(state["pull_s"], end_s)
+    yield
     d_val_s = split(d_val)
     strict = rows // MB > columns // MB
     d_lower = jnp.where(strict, dot(d_val_s, state["rate_res_s"], (1, 1)), 0.0)
+    yield
     d_gram_s = split(d_lower + d_lower.T)
     d_keys = (
         state["from_scores"]
@@ -148,6 +192,7 @@
         + dot(state["rate_res_s"], end_s, (1, 1))
         - dot(d_gram_s, state["keys_s"])
     )
+    yield
     keys = state["keys"]
     d_raw = state["norm_inv"] * (d_keys - keys * jnp.sum(keys * d_keys, axis=1, keepdims=True))
     d_rate = jnp.sum(state["residual"] * d_val, axis=1, keepdims=True) / state["rate"]
@@ -160,8 +205,8 @@
     sizes,
     tok_ref, w_ref, init_ref, rates_ref, gate_ref, gain_ref, cot_ref,
     gt_out, proj_out, ext_out, gates_out,
-    tok_t, maps, maps_all, pulls, pulls_all, acc, ext, full, ext_full, landing, ext_landing, part, part_in,
-    maps_send, maps_recv, pulls_send, pulls_recv, part_send, part_recv, red_send, red_recv, done_sem,
+    tok_t, maps, maps_all, pulls, pulls_all, acc, ext, landing, ext_landing, part, part_in,
+    maps_send, maps_recv, pulls_send, pulls_recv, part_send, part_recv, red_send, red_recv,
 ):
     n_dp, n_ctx, n_head = sizes
     count, model = tok_ref.shape
@@ -193,16 +238,17 @@
     ]
     span = [slice(h * width, (h + 1) * width) for h in range(heads)]
     queries = [projected[0][:, s] for s in span]
-    states = []
     rows, columns = grid_index(width)
     eye = jnp.where(rows == columns, 1.0, 0.0)
-    for h in range(heads):
-        state = prepare(
+    states = together([
+        prepare(
             queries[h], projected[1][:, span[h]], projected[2][:, span[h]], rates_ref[h], gate_ref[0, h : h + 1, :]
         )
-        states.append(state)
-        maps[h, 0] = eye - state["ends"][:, width:]
-        maps[h, 1] = state["ends"][:, :width]
+        for h in range(heads)
+    ])
+    for h in range(heads):
+        maps[h, 0] = eye - states[h]["ends"][:, width:]
+        maps[h, 1] = states[h]["ends"][:, :width]
 
     pl.semaphore_wait(barrier, (n_ctx - 1) + (n_head - 1) + len(dp_bits))
 
@@ -219,26 +265,27 @@
         return copies
 
     copies = share(maps, maps_all, maps_send, maps_recv)
-    for h in range(heads):
-        reach_out(queries[h], states[h])
+    together([reach_out(queries[h], states[h]) for h in range(heads)])
     tok_t[...] = tokens.T
     for copy in copies:
         copy.wait()
 
-    upstreams = []
+    starts = [init_ref[h] for h in range(heads)]
+    for i in range(n_ctx - 1):
+        for h in range(heads):
+            moved = dot(split(maps_all[i, h, 0]), split(starts[h])) + maps_all[i, h, 1]
+            starts[h] = jnp.where(ctx > i, moved, starts[h])
+    upstreams = [cot_ref[:, span[h]].astype(F32) for h in range(heads)]
+    pulled = together([
+        forward(starts[h], gain_ref[h : h + 1, :], upstreams[h], states[h]) for h in range(heads)
+    ])
     for h in range(heads):
-        start = init_ref[h]
-        for i in range(n_ctx - 1):
-            moved = dot(split(maps_all[i, h, 0]), split(start)) + maps_all[i, h, 1]
-            start = jnp.where(ctx > i, moved, start)
-        upstream = cot_ref[:, span[h]].astype(F32)
-        upstreams.append(upstream)
-        pulls[h] = forward(start, gain_ref[h : h + 1, :], upstream, states[h])
+        pulls[h] = pulled[h]
     copies = share(pulls, pulls_all, pulls_send, pulls_recv)
 
     half = model // 2
-    work = [(which * 2 + part_, acc, full, landing, (which * 2 + part_) * half, half, orders[part_]) for which in range(3) for part_ in range(2)]
-    work.append((6, ext, ext_full, ext_landing, 0, ext.shape[0], orders[0]))
+    work = [(which * 2 + part_, acc, proj_out, landing, (which * 2 + part_) * half, half, orders[part_]) for which in range(3) for part_ in range(2)]
+    work.append((6, ext, ext_out, ext_landing, 0, ext.shape[0], orders[0]))
     at = {item[0]: item[4] for item in work}
     flight = {}
 
@@ -288,82 +335,97 @@
             reduce_start(work[which * 2 + part_], 0)
         return grad
 
+    def advance(item, turn):
+        if turn < stages:
+            reduce_end(item, turn)
+        else:
+            flight[item[0]][0].wait()
+        if turn + 1 < stages:
+            reduce_start(item, turn + 1)
+        elif turn + 1 < 2 * stages:
+            gather_start(item, 2 * stages - 2 - turn)
+
+    share_ = model // n_head
     d_rows = [None] * 3
-    d_rows[0] = project(0, [query_grad(queries[h], upstreams[h], states[h]) for h in range(heads)])
-    for h in range(heads):
-        before_end(queries[h], states[h])
+
+    def token_part(which_head, which):
+        weight = w_ref[which, pl.ds(pl.multiple_of(which_head * share_, share_), share_), :]
+        return lax.dot_general(d_rows[which], weight, (((1,), (1,)), ((), ())), preferred_element_type=F32)
+
+    targets = [lax.rem(head + off, n_head) for off in range(1, n_head)]
+    d_rows[0] = project(0, together([query_grad(queries[h], upstreams[h], states[h]) for h in range(heads)]))
+    together([before_end(queries[h], states[h]) for h in range(heads)])
+    for n, to in enumerate(targets):
+        part[n] = token_part(to, 0)
     for copy in copies:
         copy.wait()
-
-    results = []
-    ext[...] = jnp.zeros_like(ext)
-    for h in range(heads):
-        grad = jnp.zeros((width, width), F32)
-        end_grad = grad
-        for i in reversed(range(n_ctx)):
-            end_grad = jnp.where(ctx == i, grad, end_grad)
-            grad = dot(split(maps_all[i, h, 0]), split(grad), (0, 0)) + pulls_all[i, h]
-        ext[0:width, span[h]] = jnp.where(ctx == 0, grad, 0.0)
-        d_raw, d_val, gates, d_base = key_value_grad(end_grad, rates_ref[h], gate_ref[0, h : h + 1, :], states[h])
-        results.append((d_raw, d_val))
-        gates_out[0, h : h + 1, :] = gates
-        ext[width : width + 1, span[h]] = states[h]["d_gain"]
-        ext[width + 8 : width + 9, span[h]] = jnp.broadcast_to(d_base, (1, width))
+    for item in work[:2]:
+        advance(item, 0)
+
+    grads = [jnp.zeros((width, width), F32)] * heads
+    end_grads = list(grads)
+    for i in reversed(range(n_ctx)):
+        for h in range(heads):
+            end_grads[h] = jnp.where(ctx == i, grads[h], end_grads[h])
+            grads[h] = dot(split(maps_all[i, h, 0]), split(grads[h]), (0, 0)) + pulls_all[i, h]
+    results = together([
+        key_value_grad(end_grads[h], rates_ref[h], gate_ref[0, h : h + 1, :], states[h]) for h in range(heads)
+    ])
     d_rows[1] = project(1, [r[0] for r in results])
     d_rows[2] = project(2, [r[1] for r in results])
-    reduce_start(work[6], 0)
-
-    share_ = model // n_head
-
-    def token_part(which_head):
-        total = None
-        for which in range(3):
-            weight = w_ref[which, pl.ds(pl.multiple_of(which_head * share_, share_), share_), :]
-            term = lax.dot_general(d_rows[which], weight, (((1,), (1,)), ((), ())), preferred_element_type=F32)
-            total = term if total is None else total + term
-        return total
+    for item in work[:2]:
+        advance(item, 1)
 
     part_copies = []
-    for off in range(1, n_head):
-        to = lax.rem(head + off, n_head)
-        part[off - 1] = token_part(to)
+    for n, to in enumerate(targets):
+        part[n] = part[n] + token_part(to, 1) + token_part(to, 2)
         copy = pltpu.make_async_remote_copy(
-            src_ref=part.at[off - 1], dst_ref=part_in.at[off - 1],
-            send_sem=part_send.at[off - 1], recv_sem=part_recv.at[off - 1],
+            src_ref=part.at[n], dst_ref=part_in.at[n], send_sem=part_send.at[n], recv_sem=part_recv.at[n],
             device_id={"head": to}, device_id_type=MESH,
         )
         copy.start()
         part_copies.append(copy)
-    own_part = token_part(head)
-
-    for stage in range(stages):
-        for item in work:
-            reduce_end(item, stage)
-            if stage + 1 < stages:
-                reduce_start(item, stage + 1)
-            else:
-                gather_start(item, stage)
-    for stage in reversed(range(stages - 1)):
-        for item in work:
-            flight[item[0]][0].wait()
-            gather_start(item, stage)
-    for copy in part_copies:
-        copy.wait()
-    for off in range(1, n_head):
-        own_part = own_part + part_in[off - 1]
-    gt_out[...] = own_part.astype(BF16)
-    outs = []
-    for item in work:
-        number, _, target, _, base, length, _ = item
-        flight[number][0].wait()
-        if number < 6:
-            copy = pltpu.make_async_copy(target.at[pl.ds(base, length)], proj_out.at[pl.ds(base, length)], done_sem.at[number])
-            copy.start()
-            outs.append(copy)
-        else:
-            ext_out[...] = ext_full[...]
-    for copy in outs:
-        copy.wait()
+    for item in work[2:6]:
+        advance(item, 0)
+
+    ext[...] = jnp.zeros_like(ext)
+    for h in range(heads):
+        ext[0:width, span[h]] = jnp.where(ctx == 0, grads[h], 0.0)
+        gates_out[0, h : h + 1, :] = results[h][2]
+        ext[width : width + 1, span[h]] = states[h]["d_gain"]
+        ext[width + 8 : width + 9, span[h]] = jnp.broadcast_to(results[h][3], (1, width))
+    reduce_start(work[6], 0)
+    own_part = token_part(head, 0) + token_part(head, 1) + token_part(head, 2)
+
+    last = 2 * stages - 1
+    for turn in range(1, last + 1):
+        if turn < last:
+            for item in work[:2]:
+                advance(item, turn + 1)
+        for item in work[2:6]:
+            advance(item, turn)
+        advance(work[6], turn - 1)
+        if turn == last - 1:
+            for copy in part_copies:
+                copy.wait()
+            for n in range(n_head - 1):
+                own_part = own_part + part_in[n]
+            gt_out[...] = own_part.astype(BF16)
+    advance(work[6], last)
+
+
+def finish_kernel(gt_in, proj_in, ext_in, gates_in, gt_out, proj_out, init_out, gain_out, rates_out, gates_out, sem):
+    copy = pltpu.make_async_copy(proj_in, proj_out, sem)
+    copy.start()
+    heads, width, _ = init_out.shape
+    gt_out[...] = gt_in[...]
+    gates_out[...] = gates_in[...]
+    for h in range(heads):
+        span = slice(h * width, (h + 1) * width)
+        init_out[h] = ext_in[0:width, span]
+        gain_out[h : h + 1, :] = ext_in[width : width + 1, span]
+        rates_out[h : h + 1, :] = ext_in[width + 8 : width + 9, h * width : h * width + 1]
+    copy.wait()
 
 
 def body(sizes, tokens, proj_weights, init_weight, base_rates, gate_values, out_gain, cotangent):
@@ -379,13 +441,13 @@
     tokens_grad, proj, ext, gates = pl.pallas_call(
         functools.partial(kernel, sizes),
         out_shape=(
-            jax.ShapeDtypeStruct((count, model // n_head), BF16),
-            jax.ShapeDtypeStruct((3 * model, span), F32),
-            jax.ShapeDtypeStruct((ext_rows, span), F32),
-            jax.ShapeDtypeStruct(gate_values.shape, F32),
+            vmem((count, model // n_head), BF16),
+            vmem((3 * model, span), F32),
+            vmem((ext_rows, span), F32),
+            vmem(gate_values.shape, F32),
         ),
         in_specs=[in_vmem] * 3 + [pl.BlockSpec(memory_space=pltpu.SMEM)] + [in_vmem] * 3,
-        out_specs=(in_vmem, pl.BlockSpec(memory_space=pl.ANY), in_vmem, in_vmem),
+        out_specs=(in_vmem,) * 4,
         scratch_shapes=[
             vmem((model, count), BF16),
             vmem((heads, 2, width, width), F32),
@@ -396,27 +458,38 @@
             vmem((ext_rows, span), F32),
             vmem((3 * model, span), F32),
             vmem((ext_rows, span), F32),
-            vmem((3 * model, span), F32),
-            vmem((ext_rows, span), F32),
             vmem((n_head - 1, count, model // n_head), F32),
             vmem((n_head - 1, count, model // n_head), F32),
             dma((n_ctx - 1,)), dma((n_ctx - 1,)), dma((n_ctx - 1,)), dma((n_ctx - 1,)),
             dma((n_head - 1,)), dma((n_head - 1,)),
-            dma((7, 2 * stages)), dma((7, 2 * stages)), dma((6,)),
+            dma((7, 2 * stages)), dma((7, 2 * stages)),
         ],
         compiler_params=pltpu.CompilerParams(
-            collective_id=0, has_side_effects=True, vmem_limit_bytes=56 * 1024 * 1024
+            collective_id=0, has_side_effects=True, vmem_limit_bytes=44 * 1024 * 1024
         ),
         cost_estimate=pl.CostEstimate(flops=4_000_000_000, bytes_accessed=12_000_000, transcendentals=0),
     )(
         flattened, proj_weights, init_weight, base_rates, gate_values, out_gain,
         cotangent.reshape(count, span),
     )
-    grad_init = jnp.stack([ext[:width, h * width : (h + 1) * width] for h in range(heads)])
-    grad_gain = ext[width].reshape(heads, width)
-    grad_rates = ext[width + 8].reshape(heads, width)[:, 0]
+    anywhere = pl.BlockSpec(memory_space=pl.ANY)
+    tokens_grad, proj, grad_init, grad_gain, grad_rates, gates = pl.pallas_call(
+        finish_kernel,
+        out_shape=(
+            jax.ShapeDtypeStruct((count, model // n_head), BF16),
+            jax.ShapeDtypeStruct((3 * model, span), F32),
+            jax.ShapeDtypeStruct(init_weight.shape, F32),
+            jax.ShapeDtypeStruct(out_gain.shape, F32),
+            jax.ShapeDtypeStruct((heads, 1), F32),
+            jax.ShapeDtypeStruct(gate_values.shape, F32),
+        ),
+        in_specs=[in_vmem, anywhere, in_vmem, in_vmem],
+        out_specs=(in_vmem, anywhere, in_vmem, in_vmem, in_vmem, in_vmem),
+        scratch_shapes=[dma],
+        cost_estimate=pl.CostEstimate(flops=0, bytes_accessed=8_000_000, transcendentals=0),
+    )(tokens_grad, proj, ext, gates)
     return (
-        tokens_grad[None], proj.reshape(3, model, span), grad_init, grad_gain, grad_rates, gates,
+        tokens_grad[None], proj.reshape(3, model, span), grad_init, grad_gain, grad_rates[:, 0], gates,
     )
 
 

time: 110 us -> 295 us (2.68)
  Pallas kernels: 97.1 us -> 283 us
    pallas_call x1 -> x2, Pallas kernels: 97.1 us -> 283 us  [the longest x1 193 us: body(): pl.pallas_call(finish_kernel, out_shape=(jax.ShapeDtypeStruct((count, mod...]
    unnamed x6 -> x20, local copies, waits for them, and re-layouts: 8.74 us -> 9.69 us
where the time goes in v1:
time: 295 us
  Pallas kernels  283 us (96%)
  local copies, waits for them, and re-layouts  9.69 us (3%)
    pallas_call x1, Pallas kernels, body(): pl.pallas_call(finish_kernel, out_shape=(jax.ShapeDtypeStruct((count, mod...  193 us
    pallas_call x1, Pallas kernels, body(): pl.pallas_call(functools.partial(kernel, sizes), out_shape=(vmem((count,...  89.8 us
    unnamed x20, local copies, waits for them, and re-layouts  9.69 us

profile of v1, /device:TPU:0, one launch (start us, length us, event | category | flops | bytes accessed | tf_op | source)
XLA Modules:
  0.0 294.9 jit_solution(1766045579564085251)
XLA Ops:
  0.6 0.0 copy-start.4
  0.6 1.2 copy-done.4
  1.9 0.0 copy-start.5
  1.9 0.9 copy-done.5
  2.8 0.0 copy-start.6
  2.8 0.9 copy-done.6
  3.7 0.0 copy-start.7
  3.7 0.7 copy-done.7
  4.4 0.0 copy-start.8
  4.4 0.7 copy-done.8
  5.0 0.0 copy-start.9
  5.0 0.7 copy-done.9
  5.7 89.8 %shard_map.118 = (bf16[256,512]{1,0:T(8,128)(2,1)S(1)}, f32[6144,256]{1,0:T(8,128)S(1)}, f32[256,256]{1,0:T(8,128)S(1)}, f32[1,2,256]{2,1,0:T(2,128)S(1)}) custom-call(bf16[256,2048]{1,0:T(8,128)(2,1)S(1)} %bitcast.4, bf16[3,2048,256]{2,1,0:T(8,128)(2,1)} %w_ref.1, f32[2,128,128]{2,1,0:T(8,128)S(1)} %copy-done.5, f32[2]{0:T(128)S(1)} %copy-done.9, ...), custom_call_target="tpu_custom_call" | custom-call | flops 4000000000 | bytes 12000000 | tf_op jit(solution)/shard_map/pallas_call | solution.py:441
  95.5 0.0 copy-start
  95.5 2.7 copy-done
  98.2 0.0 copy-start.1
  98.2 0.7 copy-done.1
  98.9 0.0 copy-start.2
  98.9 0.7 copy-done.2
  99.6 0.0 copy-start.3
  99.6 0.6 copy-done.3
  100.2 193.5 %shard_map.119 = (bf16[256,512]{1,0:T(8,128)(2,1)}, f32[6144,256]{1,0:T(8,128)}, f32[2,128,128]{2,1,0:T(8,128)}, f32[2,128]{1,0:T(2,128)}, f32[2,1]{1,0:T(2,128)}, /*index=5*/f32[1,2,256]{2,1,0:T(2,128)}) custom-call(bf16[256,512]{1,0:T(8,128)(2,1)} %copy-done.1, f32[6144,256]{1,0:T(8,128)} %copy-done, f32[256,256]{1,0:T(8,128)} %copy-done.2, ...), custom_call_target="tpu_custom_call" | custom-call | bytes 8000000 | tf_op jit(solution)/shard_map/pallas_call | solution.py:476
  293.6 1.3 reduce
Async XLA Ops:
  0.6 1.2 copy-start.4
  1.9 0.9 copy-start.5
  2.8 0.9 copy-start.6
  3.7 0.7 copy-start.7
  4.4 0.7 copy-start.8
  5.0 0.7 copy-start.9
  95.5 2.7 copy-start
  98.2 0.7 copy-start.1
  98.9 0.7 copy-start.2
  99.6 0.6 copy-start.3

commit v2 on v1

--- a/solution.py
+++ b/solution.py
@@ -20,16 +20,21 @@
     return (high, (x - high.astype(F32)).astype(BF16))
 
 
+def flipped(x):
+    return tuple(None if piece is None else piece.T for piece in x)
+
+
 def dot(left, right, dims=(1, 0)):
-    def one(a, b):
-        return lax.dot_general(a, b, (((dims[0],), (dims[1],)), ((), ())), preferred_element_type=F32)
-
-    total = one(left[0], right[0])
+    if dims[0] == 0:
+        return dot(flipped(left), right, (1, dims[1]))
+    terms = [(left[0], right[0])]
     if right[1] is not None:
-        total = total + one(left[0], right[1])
+        terms.append((left[0], right[1]))
     if left[1] is not None:
-        total = total + one(left[1], right[0])
-    return total
+        terms.append((left[1], right[0]))
+    a = jnp.concatenate([t[0] for t in terms], axis=1)
+    b = jnp.concatenate([t[1] for t in terms], axis=dims[1])
+    return lax.dot_general(a, b, (((1,), (dims[1],)), ((), ())), preferred_element_type=F32)
 
 
 def together(steps):
@@ -130,7 +135,8 @@
     state["scores_s"] = split(scores)
     state["reach_s"] = split(queries.astype(F32) - mixed[:, width:])
     state["own_out"] = mixed[:, :width]
-    state["pull_s"] = split(dot(state["inverse_s"], state["rate_keys_s"], (0, 0)))
+    state["inverse_t"] = flipped(state["inverse_s"])
+    state["pull_s"] = split(dot(state["inverse_t"], state["rate_keys_s"]))
 
 
 def forward(start, gain, upstream, state):
@@ -173,7 +179,7 @@
     yield
     pushed = state["rate"] * dot(state["scores_s"], state["d_out_s"], (0, 0))
     yield
-    state["d_val"] = dot(state["inverse_s"], split(pushed), (0, 0))
+    state["d_val"] = dot(state["inverse_t"], split(pushed))
 
 
 def key_value_grad(end_grad, base, gate_row, state):
@@ -203,16 +209,19 @@
 
 def kernel(
     sizes,
-    tok_ref, w_ref, init_ref, rates_ref, gate_ref, gain_ref, cot_ref,
+    tok_ref, w_hbm, init_ref, rates_ref, gate_ref, gain_ref, cot_ref,
     gt_out, proj_out, ext_out, gates_out,
-    tok_t, maps, maps_all, pulls, pulls_all, acc, ext, landing, ext_landing, part, part_in,
-    maps_send, maps_recv, pulls_send, pulls_recv, part_send, part_recv, red_send, red_recv,
+    w_ref, tok_t, maps, maps_all, pulls, pulls_all, acc, ext, landing, ext_landing, part, part_in,
+    maps_send, maps_recv, pulls_send, pulls_recv, part_send, part_recv, red_send, red_recv, w_sem,
 ):
     n_dp, n_ctx, n_head = sizes
     count, model = tok_ref.shape
     heads, width, _ = init_ref.shape
     dp, ctx, head = lax.axis_index("dp"), lax.axis_index("ctx"), lax.axis_index("head")
     place = {"dp": dp, "ctx": ctx}
+    w_copies = [pltpu.make_async_copy(w_hbm.at[which], w_ref.at[which], w_sem.at[which]) for which in (1, 2, 0)]
+    for copy in w_copies:
+        copy.start()
 
     def flip(axis, bit):
         step = 1 << bit
@@ -233,9 +242,10 @@
         pl.semaphore_signal(barrier, inc=1, device_id={axis: flip(axis, bit)[1]}, device_id_type=MESH)
 
     tokens = tok_ref[...]
-    projected = [
-        jnp.dot(tokens, w_ref[which], preferred_element_type=F32).astype(BF16) for which in range(3)
-    ]
+    projected = [None] * 3
+    for which in (1, 2, 0):
+        w_copies[(1, 2, 0).index(which)].wait()
+        projected[which] = jnp.dot(tokens, w_ref[which], preferred_element_type=F32).astype(BF16)
     span = [slice(h * width, (h + 1) * width) for h in range(heads)]
     queries = [projected[0][:, s] for s in span]
     rows, columns = grid_index(width)
@@ -424,7 +434,7 @@
         span = slice(h * width, (h + 1) * width)
         init_out[h] = ext_in[0:width, span]
         gain_out[h : h + 1, :] = ext_in[width : width + 1, span]
-        rates_out[h : h + 1, :] = ext_in[width + 8 : width + 9, h * width : h * width + 1]
+        rates_out[h] = jnp.max(ext_in[width + 8 : width + 9, span])
     copy.wait()
 
 
@@ -446,9 +456,10 @@
             vmem((ext_rows, span), F32),
             vmem(gate_values.shape, F32),
         ),
-        in_specs=[in_vmem] * 3 + [pl.BlockSpec(memory_space=pltpu.SMEM)] + [in_vmem] * 3,
+        in_specs=[in_vmem, pl.BlockSpec(memory_space=pltpu.HBM), in_vmem] + [pl.BlockSpec(memory_space=pltpu.SMEM)] + [in_vmem] * 3,
         out_specs=(in_vmem,) * 4,
         scratch_shapes=[
+            vmem(proj_weights.shape, BF16),
             vmem((model, count), BF16),
             vmem((heads, 2, width, width), F32),
             vmem((n_ctx, heads, 2, width, width), F32),
@@ -462,16 +473,19 @@
             vmem((n_head - 1, count, model // n_head), F32),
             dma((n_ctx - 1,)), dma((n_ctx - 1,)), dma((n_ctx - 1,)), dma((n_ctx - 1,)),
             dma((n_head - 1,)), dma((n_head - 1,)),
-            dma((7, 2 * stages)), dma((7, 2 * stages)),
+            dma((7, 2 * stages)), dma((7, 2 * stages)), dma((3,)),
         ],
         compiler_params=pltpu.CompilerParams(
             collective_id=0, has_side_effects=True, vmem_limit_bytes=44 * 1024 * 1024
         ),
         cost_estimate=pl.CostEstimate(flops=4_000_000_000, bytes_accessed=12_000_000, transcendentals=0),
-    )(
-        flattened, proj_weights, init_weight, base_rates, gate_values, out_gain,
-        cotangent.reshape(count, span),
-    )
+    )(*(
+        pltpu.with_memory_space_constraint(x, pltpu.HBM)
+        for x in (
+            flattened, proj_weights, init_weight, base_rates, gate_values, out_gain,
+            cotangent.reshape(count, span),
+        )
+    ))
     anywhere = pl.BlockSpec(memory_space=pl.ANY)
     tokens_grad, proj, grad_init, grad_gain, grad_rates, gates = pl.pallas_call(
         finish_kernel,
@@ -480,16 +494,17 @@
             jax.ShapeDtypeStruct((3 * model, span), F32),
             jax.ShapeDtypeStruct(init_weight.shape, F32),
             jax.ShapeDtypeStruct(out_gain.shape, F32),
-            jax.ShapeDtypeStruct((heads, 1), F32),
+            jax.ShapeDtypeStruct((heads,), F32),
             jax.ShapeDtypeStruct(gate_values.shape, F32),
         ),
-        in_specs=[in_vmem, anywhere, in_vmem, in_vmem],
-        out_specs=(in_vmem, anywhere, in_vmem, in_vmem, in_vmem, in_vmem),
+        in_specs=[in_vmem] * 4,
+        out_specs=(in_vmem, anywhere, in_vmem, in_vmem, pl.BlockSpec(memory_space=pltpu.SMEM), in_vmem),
         scratch_shapes=[dma],
+        compiler_params=pltpu.CompilerParams(vmem_limit_bytes=12 * 1024 * 1024),
         cost_estimate=pl.CostEstimate(flops=0, bytes_accessed=8_000_000, transcendentals=0),
-    )(tokens_grad, proj, ext, gates)
+    )(*(pltpu.with_memory_space_constraint(x, pltpu.VMEM) for x in (tokens_grad, proj, ext, gates)))
     return (
-        tokens_grad[None], proj.reshape(3, model, span), grad_init, grad_gain, grad_rates[:, 0], gates,
+        tokens_grad[None], proj.reshape(3, model, span), grad_init, grad_gain, grad_rates, gates,
     )
 
 

time: 295 us -> 94.6 us (0.32)
  Pallas kernels: 283 us -> 93.8 us
  local copies, waits for them, and re-layouts: 9.69 us -> 0 us
    pallas_call x1, Pallas kernels: 193 us -> 3.47 us  [body(): pl.pallas_call(finish_kernel, out_shape=(jax.ShapeDtypeStruct((count, mod...]
    unnamed x20 -> x0, local copies, waits for them, and re-layouts: 9.69 us -> none
where the time goes in v2:
time: 94.6 us; the launch traced here: 94.5 us
  Pallas kernels  93.8 us (99%)
    pallas_call x1, Pallas kernels, body(): pl.pallas_call(functools.partial(kernel, sizes), out_shape=(vmem((count,...  90.3 us
    pallas_call x1, Pallas kernels, body(): pl.pallas_call(finish_kernel, out_shape=(jax.ShapeDtypeStruct((count, mod...  3.47 us

profile of v2, /device:TPU:0, one launch (start us, length us, event | category | flops | bytes accessed | tf_op | source)
XLA Modules:
  0.0 94.5 jit_solution(4188465474546255560)
XLA Ops:
  0.6 90.3 %shard_map.118 = (bf16[256,512]{1,0:T(8,128)(2,1)S(1)}, f32[6144,256]{1,0:T(8,128)S(1)}, f32[256,256]{1,0:T(8,128)S(1)}, f32[1,2,256]{2,1,0:T(2,128)S(1)}) custom-call(bf16[256,2048]{1,0:T(8,128)(2,1)} %bitcast.5, bf16[3,2048,256]{2,1,0:T(8,128)(2,1)} %w_hbm.1, f32[2,128,128]{2,1,0:T(8,128)} %init_ref.1, f32[2]{0:T(128)} %rates_ref.1, ...), custom_call_target="tpu_custom_call" | custom-call | flops 4000000000 | bytes 12000000 | tf_op jit(solution)/shard_map/pallas_call | solution.py:451
  91.0 3.5 %shard_map.119 = (bf16[256,512]{1,0:T(8,128)(2,1)}, f32[6144,256]{1,0:T(8,128)}, f32[2,128,128]{2,1,0:T(8,128)}, f32[2,128]{1,0:T(2,128)}, f32[2]{0:T(128)}, /*index=5*/f32[1,2,256]{2,1,0:T(2,128)}) custom-call(bf16[256,512]{1,0:T(8,128)(2,1)S(1)} %get-tuple-element.16.gt_in, f32[6144,256]{1,0:T(8,128)S(1)} %get-tuple-element.17.proj_in, ...), custom_call_target="tpu_custom_call" | custom-call | bytes 8000000 | tf_op jit(solution)/shard_map/pallas_call | solution.py:490

commit v3 on v2

--- a/solution.py
+++ b/solution.py
@@ -211,8 +211,8 @@
     sizes,
     tok_ref, w_hbm, init_ref, rates_ref, gate_ref, gain_ref, cot_ref,
     gt_out, proj_out, ext_out, gates_out,
-    w_ref, tok_t, maps, maps_all, pulls, pulls_all, acc, ext, landing, ext_landing, part, part_in,
-    maps_send, maps_recv, pulls_send, pulls_recv, part_send, part_recv, red_send, red_recv, w_sem,
+    w_ref, tok_t, maps, maps_all, pulls, pulls_all, acc, ext, landing, ext_landing, part, from_low, from_high,
+    maps_send, maps_recv, pulls_send, pulls_recv, up_send, up_recv, down_send, down_recv, red_send, red_recv, w_sem,
 ):
     n_dp, n_ctx, n_head = sizes
     count, model = tok_ref.shape
@@ -359,18 +359,51 @@
     d_rows = [None] * 3
 
     def token_part(which_head, which):
-        weight = w_ref[which, pl.ds(pl.multiple_of(which_head * share_, share_), share_), :]
+        weight = w_ref[which, which_head * share_ : (which_head + 1) * share_, :]
         return lax.dot_general(d_rows[which], weight, (((1,), (1,)), ((), ())), preferred_element_type=F32)
 
-    targets = [lax.rem(head + off, n_head) for off in range(1, n_head)]
+    def upward(j):
+        return pltpu.make_async_remote_copy(
+            src_ref=part.at[j], dst_ref=from_low.at[j], send_sem=up_send.at[j], recv_sem=up_recv.at[j],
+            device_id={"head": lax.rem(head + 1, n_head)}, device_id_type=MESH,
+        )
+
+    def downward(j):
+        return pltpu.make_async_remote_copy(
+            src_ref=part.at[j], dst_ref=from_high.at[j], send_sem=down_send.at[j], recv_sem=down_recv.at[j],
+            device_id={"head": lax.rem(head + n_head - 1, n_head)}, device_id_type=MESH,
+        )
+
+    def pass_on(turn):
+        for j in range(n_head):
+            low = turn - (n_head - 1 - j)
+            if 1 <= low <= j:
+
+                @pl.when(head == low)
+                def _():
+                    upward(j).wait_recv()
+                    if low < j:
+                        part[j] = part[j] + from_low[j]
+                        upward(j).start()
+
+            high = n_head - 1 - (turn - j)
+            if j <= high <= n_head - 2:
+
+                @pl.when(head == high)
+                def _():
+                    downward(j).wait_recv()
+                    if high > j:
+                        part[j] = part[j] + from_high[j]
+                        downward(j).start()
+
     d_rows[0] = project(0, together([query_grad(queries[h], upstreams[h], states[h]) for h in range(heads)]))
     together([before_end(queries[h], states[h]) for h in range(heads)])
-    for n, to in enumerate(targets):
-        part[n] = token_part(to, 0)
+    for j in range(n_head):
+        part[j] = token_part(j, 0)
+    for item in work[:2]:
+        advance(item, 0)
     for copy in copies:
         copy.wait()
-    for item in work[:2]:
-        advance(item, 0)
 
     grads = [jnp.zeros((width, width), F32)] * heads
     end_grads = list(grads)
@@ -386,16 +419,22 @@
     for item in work[:2]:
         advance(item, 1)
 
-    part_copies = []
-    for n, to in enumerate(targets):
-        part[n] = part[n] + token_part(to, 1) + token_part(to, 2)
-        copy = pltpu.make_async_remote_copy(
-            src_ref=part.at[n], dst_ref=part_in.at[n], send_sem=part_send.at[n], recv_sem=part_recv.at[n],
-            device_id={"head": to}, device_id_type=MESH,
-        )
-        copy.start()
-        part_copies.append(copy)
-    for item in work[2:6]:
+    for item in work[2:4]:
+        advance(item, 0)
+    for j in range(n_head):
+        part[j] = part[j] + token_part(j, 1) + token_part(j, 2)
+
+    @pl.when(head == 0)
+    def _():
+        for j in range(n_head - 1, 0, -1):
+            upward(j).start()
+
+    @pl.when(head == n_head - 1)
+    def _():
+        for j in range(n_head - 1):
+            downward(j).start()
+
+    for item in work[4:6]:
         advance(item, 0)
 
     ext[...] = jnp.zeros_like(ext)
@@ -405,9 +444,8 @@
         ext[width : width + 1, span[h]] = states[h]["d_gain"]
         ext[width + 8 : width + 9, span[h]] = jnp.broadcast_to(results[h][3], (1, width))
     reduce_start(work[6], 0)
-    own_part = token_part(head, 0) + token_part(head, 1) + token_part(head, 2)
-
     last = 2 * stages - 1
+    passed = 0
     for turn in range(1, last + 1):
         if turn < last:
             for item in work[:2]:
@@ -415,12 +453,30 @@
         for item in work[2:6]:
             advance(item, turn)
         advance(work[6], turn - 1)
-        if turn == last - 1:
-            for copy in part_copies:
-                copy.wait()
-            for n in range(n_head - 1):
-                own_part = own_part + part_in[n]
-            gt_out[...] = own_part.astype(BF16)
+        if turn in (1, 3, 4):
+            passed += 1
+            pass_on(passed)
+    for turn in range(passed + 1, n_head):
+        pass_on(turn)
+    for j in range(n_head):
+
+        @pl.when(head == j)
+        def _():
+            total = part[j]
+            if j > 0:
+                total = total + from_low[j]
+            if j < n_head - 1:
+                total = total + from_high[j]
+            gt_out[...] = total.astype(BF16)
+
+        @pl.when(head < j)
+        def _():
+            upward(j).wait_send()
+
+        @pl.when(head > j)
+        def _():
+            downward(j).wait_send()
+
     advance(work[6], last)
 
 
@@ -469,10 +525,11 @@
             vmem((ext_rows, span), F32),
             vmem((3 * model, span), F32),
             vmem((ext_rows, span), F32),
-            vmem((n_head - 1, count, model // n_head), F32),
-            vmem((n_head - 1, count, model // n_head), F32),
+            vmem((n_head, count, model // n_head), F32),
+            vmem((n_head, count, model // n_head), F32),
+            vmem((n_head, count, model // n_head), F32),
             dma((n_ctx - 1,)), dma((n_ctx - 1,)), dma((n_ctx - 1,)), dma((n_ctx - 1,)),
-            dma((n_head - 1,)), dma((n_head - 1,)),
+            dma((n_head,)), dma((n_head,)), dma((n_head,)), dma((n_head,)),
             dma((7, 2 * stages)), dma((7, 2 * stages)), dma((3,)),
         ],
         compiler_params=pltpu.CompilerParams(

time: 94.6 us -> 93.7 us (level)
  no operation moved by 1% of the time
where the time goes in v3:
time: 93.7 us; the launch traced here: 93.6 us
  Pallas kernels  92.9 us (99%)
    pallas_call x1, Pallas kernels, body(): pl.pallas_call(functools.partial(kernel, sizes), out_shape=(vmem((count,...  89.5 us
    pallas_call x1, Pallas kernels, body(): pl.pallas_call(finish_kernel, out_shape=(jax.ShapeDtypeStruct((count, mod...  3.47 us

profile of v3, /device:TPU:0, one launch (start us, length us, event | category | flops | bytes accessed | tf_op | source)
XLA Modules:
  0.0 93.6 jit_solution(9211337272016862213)
XLA Ops:
  0.6 89.5 %shard_map.118 = (bf16[256,512]{1,0:T(8,128)(2,1)S(1)}, f32[6144,256]{1,0:T(8,128)S(1)}, f32[256,256]{1,0:T(8,128)S(1)}, f32[1,2,256]{2,1,0:T(2,128)S(1)}) custom-call(bf16[256,2048]{1,0:T(8,128)(2,1)} %bitcast.5, bf16[3,2048,256]{2,1,0:T(8,128)(2,1)} %w_hbm.1, f32[2,128,128]{2,1,0:T(8,128)} %init_ref.1, f32[2]{0:T(128)} %rates_ref.1, ...), custom_call_target="tpu_custom_call" | custom-call | flops 4000000000 | bytes 12000000 | tf_op jit(solution)/shard_map/pallas_call | solution.py:507
  90.1 3.5 %shard_map.119 = (bf16[256,512]{1,0:T(8,128)(2,1)}, f32[6144,256]{1,0:T(8,128)}, f32[2,128,128]{2,1,0:T(8,128)}, f32[2,128]{1,0:T(2,128)}, f32[2]{0:T(128)}, /*index=5*/f32[1,2,256]{2,1,0:T(2,128)}) custom-call(bf16[256,512]{1,0:T(8,128)(2,1)S(1)} %get-tuple-element.16.gt_in, f32[6144,256]{1,0:T(8,128)S(1)} %get-tuple-element.17.proj_in, ...), custom_call_target="tpu_custom_call" | custom-call | bytes 8000000 | tf_op jit(solution)/shard_map/pallas_call | solution.py:547

commit v4 on v3

--- a/solution.py
+++ b/solution.py
@@ -277,8 +277,9 @@
     copies = share(maps, maps_all, maps_send, maps_recv)
     together([reach_out(queries[h], states[h]) for h in range(heads)])
     tok_t[...] = tokens.T
+    sent = list(copies)
     for copy in copies:
-        copy.wait()
+        copy.wait_recv()
 
     starts = [init_ref[h] for h in range(heads)]
     for i in range(n_ctx - 1):
@@ -318,7 +319,8 @@
     def reduce_end(item, stage):
         number, source, target, land = item[:4]
         copy, slot, length = flight[number]
-        copy.wait()
+        copy.wait_recv()
+        sent.append(copy)
         total = source[pl.ds(at[number], length)] + land[pl.ds(slot, length)]
         (target if stage == stages - 1 else source)[pl.ds(at[number], length)] = total
 
@@ -349,7 +351,8 @@
         if turn < stages:
             reduce_end(item, turn)
         else:
-            flight[item[0]][0].wait()
+            flight[item[0]][0].wait_recv()
+            sent.append(flight[item[0]][0])
         if turn + 1 < stages:
             reduce_start(item, turn + 1)
         elif turn + 1 < 2 * stages:
@@ -402,8 +405,9 @@
         part[j] = token_part(j, 0)
     for item in work[:2]:
         advance(item, 0)
+    sent.extend(copies)
     for copy in copies:
-        copy.wait()
+        copy.wait_recv()
 
     grads = [jnp.zeros((width, width), F32)] * heads
     end_grads = list(grads)
@@ -478,11 +482,18 @@
             downward(j).wait_send()
 
     advance(work[6], last)
+    for copy in sent:
+        copy.wait_send()
 
 
 def finish_kernel(gt_in, proj_in, ext_in, gates_in, gt_out, proj_out, init_out, gain_out, rates_out, gates_out, sem):
-    copy = pltpu.make_async_copy(proj_in, proj_out, sem)
-    copy.start()
+    pieces = sem.shape[0]
+    rows = proj_in.shape[0] // pieces
+    copies = []
+    for n in range(pieces):
+        where = pl.ds(n * rows, rows)
+        copies.append(pltpu.make_async_copy(proj_in.at[where], proj_out.at[where], sem.at[n]))
+        copies[n].start()
     heads, width, _ = init_out.shape
     gt_out[...] = gt_in[...]
     gates_out[...] = gates_in[...]
@@ -491,7 +502,8 @@
         init_out[h] = ext_in[0:width, span]
         gain_out[h : h + 1, :] = ext_in[width : width + 1, span]
         rates_out[h] = jnp.max(ext_in[width + 8 : width + 9, span])
-    copy.wait()
+    for copy in copies:
+        copy.wait()
 
 
 def body(sizes, tokens, proj_weights, init_weight, base_rates, gate_values, out_gain, cotangent):
@@ -556,7 +568,7 @@
         ),
         in_specs=[in_vmem] * 4,
         out_specs=(in_vmem, anywhere, in_vmem, in_vmem, pl.BlockSpec(memory_space=pltpu.SMEM), in_vmem),
-        scratch_shapes=[dma],
+        scratch_shapes=[dma((6,))],
         compiler_params=pltpu.CompilerParams(vmem_limit_bytes=12 * 1024 * 1024),
         cost_estimate=pl.CostEstimate(flops=0, bytes_accessed=8_000_000, transcendentals=0),
     )(*(pltpu.with_memory_space_constraint(x, pltpu.VMEM) for x in (tokens_grad, proj, ext, gates)))

time: 93.7 us -> 92 us (0.982)
  Pallas kernels: 92.9 us -> 91.2 us
    pallas_call x1, Pallas kernels: 89.5 us -> 87.7 us  [body(): pl.pallas_call(functools.partial(kernel, sizes), out_shape=(vmem((count,...]
where the time goes in v4:
time: 92 us; the launch traced here: 91.8 us
  Pallas kernels  91.2 us (99%)
    pallas_call x1, Pallas kernels, body(): pl.pallas_call(functools.partial(kernel, sizes), out_shape=(vmem((count,...  87.7 us
    pallas_call x1, Pallas kernels, body(): pl.pallas_call(finish_kernel, out_shape=(jax.ShapeDtypeStruct((count, mod...  3.48 us

profile of v4, /device:TPU:0, one launch (start us, length us, event | category | flops | bytes accessed | tf_op | source)
XLA Modules:
  0.0 91.8 jit_solution(2319065339169543006)
XLA Ops:
  0.6 87.7 %shard_map.118 = (bf16[256,512]{1,0:T(8,128)(2,1)S(1)}, f32[6144,256]{1,0:T(8,128)S(1)}, f32[256,256]{1,0:T(8,128)S(1)}, f32[1,2,256]{2,1,0:T(2,128)S(1)}) custom-call(bf16[256,2048]{1,0:T(8,128)(2,1)} %bitcast.5, bf16[3,2048,256]{2,1,0:T(8,128)(2,1)} %w_hbm.1, f32[2,128,128]{2,1,0:T(8,128)} %init_ref.1, f32[2]{0:T(128)} %rates_ref.1, ...), custom_call_target="tpu_custom_call" | custom-call | flops 4000000000 | bytes 12000000 | tf_op jit(solution)/shard_map/pallas_call | solution.py:519
  88.3 3.5 %shard_map.119 = (bf16[256,512]{1,0:T(8,128)(2,1)}, f32[6144,256]{1,0:T(8,128)}, f32[2,128,128]{2,1,0:T(8,128)}, f32[2,128]{1,0:T(2,128)}, f32[2]{0:T(128)}, /*index=5*/f32[1,2,256]{2,1,0:T(2,128)}) custom-call(bf16[256,512]{1,0:T(8,128)(2,1)S(1)} %get-tuple-element.16.gt_in, f32[6144,256]{1,0:T(8,128)S(1)} %get-tuple-element.17.proj_in, ...), custom_call_target="tpu_custom_call" | custom-call | bytes 8000000 | tf_op jit(solution)/shard_map/pallas_call | solution.py:559
